TPU v7x, 32 devices: a whole 2x2x4 slice. The times are simulated.
32 devices in a mesh: parts: 2 (over y), dp: 4 (over x, core), group: 4 (over z).
Axes of the slice: x: 2, y: 2, z: 4, core: 2. Of those that a mesh axis runs over, the one named last changes fastest.
Arguments:
- train_hidden: bfloat16 [256, 64, 14336], P(('parts', 'dp'), None, 'group'), parts along dimension 0, may hold values from -22 to 22
- train_grad: bfloat16 [256, 64, 4096], P(('parts', 'dp'), None, 'group'), parts along dimension 0, may hold values from -8 to 8
- train_mask: int32 [256, 64], P(('parts', 'dp')), parts along dimension 0, may hold values 0 or 1
- syn_hidden: bfloat16 [128, 64, 14336], P(('parts', 'group'), None, 'dp'), parts along dimension 0, may hold values from -22 to 22
- syn_grad: bfloat16 [128, 64, 4096], P(('parts', 'group'), None, 'dp'), parts along dimension 0, may hold values from -8 to 8
- syn_mask: int32 [128, 64], P(('parts', 'group')), parts along dimension 0, may hold values 0 or 1
- basis_in: bfloat16 [14336, 64], replicated, may hold values from -0.046875 to 0.046875
- basis_out: bfloat16 [4096, 64], replicated, may hold values from -0.09375 to 0.09375
Outputs:
- scores: float32 [128, 128], P(('parts', 'group'), 'dp'), parts along dimension 0
There are 2 independent parts, one for each index of `parts`. A program takes and returns all parts, laid end to end along the dimension named above; an argument that names none is the same for every part. Nothing has to cross between parts.
All inputs are finite; a program needn't handle non-finite values. No bound on the sum of `train_mask` or of `syn_mask` on one device may be relied on, other than what follows from the above.
Results may differ from a plain program's by a relative error of at most 0.0003.
Values sent between devices are 32-bit elements; how exact they have to be, the bound alone decides.
A program may use at most 128 MiB of HBM per device.

v0:
```python
import jax
import jax.numpy as jnp
from jax import lax
from jax.sharding import PartitionSpec as P

damp_ratio = 0.1


def local_terms(hidden, grads, basis_in, basis_out, index):
    seqs, length, width = hidden.shape
    feat = grads.shape[2]
    in_rows = lax.dynamic_slice_in_dim(basis_in, index * width, width, 0)
    out_rows = lax.dynamic_slice_in_dim(basis_out, index * feat, feat, 0)
    in_proj = jnp.dot(
        hidden.reshape(seqs * length, width), in_rows, preferred_element_type=jnp.float32
    )
    out_proj = jnp.dot(
        grads.reshape(seqs * length, feat), out_rows, preferred_element_type=jnp.float32
    )
    return jnp.concatenate([in_proj, out_proj], axis=1).reshape(seqs, length, -1)


def make_codes(stacked, mask, rank):
    in_proj = stacked[:, :, :rank]
    weighted = stacked[:, :, rank:] * mask[:, :, None].astype(jnp.float32)
    codes = jnp.einsum("nta,ntb->nab", weighted, in_proj, precision=lax.Precision.HIGHEST)
    return codes.reshape(codes.shape[0], -1)


def body(train_hidden, train_grad, train_mask, syn_hidden, syn_grad, syn_mask, basis_in, basis_out):
    rank = basis_in.shape[1]
    group_pos = lax.axis_index("group")
    data_pos = lax.axis_index("dp")
    train_terms = local_terms(train_hidden, train_grad, basis_in, basis_out, group_pos)
    summed = lax.psum(train_terms, "group")
    codes = make_codes(summed, train_mask, rank)
    syn_terms = local_terms(syn_hidden, syn_grad, basis_in, basis_out, data_pos)
    syn_summed = lax.psum(syn_terms, "dp")
    syn_codes = make_codes(syn_summed, syn_mask, rank)
    width = rank * rank // lax.axis_size("group")
    columns = lax.dynamic_slice_in_dim(codes, group_pos * width, width, 1)
    every = lax.all_gather(columns, "dp", axis=0, tiled=True)
    partial_value = jnp.dot(every, every.T, precision=lax.Precision.HIGHEST)
    gram = lax.psum(partial_value, "group")
    total = gram.shape[0]
    local_count = codes.shape[0]
    damp = damp_ratio * jnp.trace(gram) / total
    system = gram + damp * jnp.eye(total, dtype=jnp.float32)
    lower = jnp.linalg.cholesky(system)
    row_ids = lax.broadcasted_iota(jnp.int32, (total, local_count), 0)
    col_ids = lax.broadcasted_iota(jnp.int32, (total, local_count), 1) + data_pos * local_count
    unit_cols = (row_ids == col_ids).astype(jnp.float32)
    first = lax.linalg.triangular_solve(lower, unit_cols, left_side=True, lower=True)
    inverse_cols = lax.linalg.triangular_solve(
        lower, first, left_side=True, lower=True, transpose_a=True
    )
    raw = jnp.dot(syn_codes, codes.T, precision=lax.Precision.HIGHEST)
    initial = jnp.zeros((raw.shape[0], local_count), jnp.float32)
    return initial + jnp.dot(
        lax.all_gather(raw, "dp", axis=1, tiled=True), inverse_cols, precision=lax.Precision.HIGHEST
    )


def solution(mesh):
    placed = (
        P(("parts", "dp"), None, "group"),
        P(("parts", "dp"), None, "group"),
        P(("parts", "dp"), None),
        P(("parts", "group"), None, "dp"),
        P(("parts", "group"), None, "dp"),
        P(("parts", "group"), None),
        P(),
        P(),
    )
    return jax.shard_map(
        body, mesh=mesh, in_specs=placed, out_specs=P(("parts", "group"), "dp"), check_vma=False
    )
```

profile of v0, /device:TPU:0, one launch (start us, length us, event | category | flops | bytes accessed | tf_op | source)
XLA Modules:
  0.0 188.8 jit_solution(6406276657698745898)
XLA Ops:
  6.5 0.0 copy-start
  6.5 0.0 all-reduce.4.cloned.1.call-start
  6.5 1.6 copy-done
  8.1 1.7 convolution_bitcast_fusion.2
  9.8 5.6 %convolution_bitcast_fusion.3 = f32[1024,64]{0,1:T(8,128)S(1)} fusion(bf16[1024,3584]{1,0:T(8,128)(2,1)} %bitcast.41, bf16[14336,64]{0,1:T(8,128)(2,1)} %param.14, s32[]{:T(128)S(6)} %select_n.22), kind=kOutput, calls=%fused_computation.3 | convolution fusion | flops 469762048 | bytes 8060932 | tf_op jit(solution)/shard_map/dot_general | solution.py:14
  15.4 1.0 copy.21
  16.4 0.0 all-reduce.4.cloned.1.call-update
  16.4 0.0 all-reduce.6.cloned.1.call-start
  16.5 0.0 copy-start.1
  16.5 10.0 %convolution_bitcast_fusion.1 = f32[2048,64]{0,1:T(8,128)S(1)} fusion(bf16[2048,3584]{1,0:T(8,128)(2,1)} %bitcast.40, bf16[14336,64]{0,1:T(8,128)(2,1)} %param.14, s32[]{:T(128)S(6)} %select_n.24), kind=kOutput, calls=%fused_computation.1 | convolution fusion | flops 939524096 | bytes 15663108 | tf_op jit(solution)/shard_map/dot_general | solution.py:14
  26.5 0.0 copy-done.1
  26.5 0.0 copy-start.2
  26.5 0.0 copy-start.3
  26.5 2.3 %convolution_bitcast_fusion = f32[2048,64]{0,1:T(8,128)S(1)} fusion(bf16[2048,1024]{1,0:T(8,128)(2,1)S(1)} %bitcast.42, bf16[4096,64]{0,1:T(8,128)(2,1)} %param.15, s32[]{:T(128)S(6)} %select_n.25), kind=kOutput, calls=%fused_computation | convolution fusion | flops 268435456 | bytes 4849668 | tf_op jit(solution)/shard_map/dot_general | solution.py:17
  28.8 0.1 pad_maximum_fusion
  28.9 1.4 copy.19
  30.3 0.0 all-reduce.6.cloned.1.call-update
  30.3 0.0 all-reduce.8.cloned.1.call-start
  30.3 0.0 copy-done.2
  30.4 0.0 copy-done.3
  30.4 21.9 %all-reduce.4.cloned.1.call-done = f32[16,64,128]{2,1,0:T(8,128)} async-done(((f32[16,64,128]{2,1,0:T(8,128)}), f32[16,64,128]{2,1,0:T(8,128)}) %all-reduce.4.cloned.1.call-update) | async-done | bytes 524304 | tf_op jit(solution)/shard_map/psum | solution.py:38
  52.4 3.3 %fusion.3 = f32[16,64,64]{2,1,0:T(8,128)} fusion(f32[16,64,128]{2,1,0:T(8,128)} %all-reduce.4.cloned.1.call-done, f32[16,64]{1,0:T(8,128)S(1)} %convert_element_type.10), kind=kOutput, calls=%fused_computation.10 | convolution fusion | flops 50397184 | bytes 1314816 | tf_op jit(solution)/shard_map/nta,ntb->nab/dot_general | solution.py:26
  55.7 50.9 %all-reduce.6.cloned.1.call-done = f32[32,64,128]{2,1,0:T(8,128)} async-done(((f32[32,64,128]{2,1,0:T(8,128)}), f32[32,64,128]{2,1,0:T(8,128)}) %all-reduce.6.cloned.1.call-update) | async-done | bytes 1048592 | tf_op jit(solution)/shard_map/psum | solution.py:35
  106.6 3.9 %fusion = f32[32,64,64]{2,1,0:T(8,128)S(1)} fusion(f32[32,64,128]{2,1,0:T(8,128)} %all-reduce.6.cloned.1.call-done, f32[32,64]{1,0:T(8,128)S(1)} %convert_element_type.11), kind=kOutput, calls=%fused_computation.5 | convolution fusion | flops 100794368 | bytes 2629632 | tf_op jit(solution)/shard_map/nta,ntb->nab/dot_general | solution.py:26
  110.5 1.1 reshape.43
  111.7 0.9 constant_dynamic-slice_fusion
  112.6 7.1 %all_gather.7 = f32[128,1024]{1,0:T(8,128)S(1)} all-gather(f32[32,1024]{1,0:T(8,128)S(1)} %constant_dynamic-slice_fusion), channel_id=1, replica_groups=mesh['parts'=2,'dp'=4,'group'=4] {'dp'}, dimensions={0}, use_global_device_ids=true | all-gather | bytes 655360 | tf_op jit(solution)/shard_map/all_gather | solution.py:42
  119.7 1.2 fusion.23
  120.9 0.0 all-reduce.8.cloned.1.call-update
  120.9 2.8 %convolution_bitcast_fusion.4 = f32[1,32,16]{1,2,0:T(8,128)S(1)} fusion(f32[32,64,64]{2,1,0:T(8,128)S(1)} %fusion, f32[16,64,64]{2,1,0:T(8,128)} %fusion.3), kind=kOutput, calls=%fused_computation.4 | convolution fusion | flops 25165824 | bytes 788480 | tf_op jit(solution)/shard_map/dot_general | solution.py:57
  123.7 5.4 %all-gather = f32[4,32,16]{1,2,0:T(8,128)S(1)} all-gather(f32[1,32,16]{1,2,0:T(8,128)S(1)} %convolution_bitcast_fusion.4), channel_id=1, replica_groups=mesh['parts'=2,'dp'=4,'group'=4] {'dp'}, dimensions={0}, use_global_device_ids=true | all-gather | bytes 10240 | tf_op jit(solution)/shard_map/all_gather | solution.py:60
  129.1 0.1 reshape.45
  129.2 25.1 %all-reduce.8.cloned.1.call-done = f32[128,128]{1,0:T(8,128)} async-done(((f32[128,128]{1,0:T(8,128)}), f32[128,128]{1,0:T(8,128)}) %all-reduce.8.cloned.1.call-update) | async-done | bytes 65552 | tf_op jit(solution)/shard_map/psum | solution.py:44
  154.3 1.5 select_reduce_fusion.1
  156.4 0.9 select_add_fusion
  157.3 0.1 copy.26
  157.4 0.9 fusion.17
  158.2 11.7 %cholesky.17 = f32[128,128]{1,0:T(8,128)S(1)} custom-call(f32[128,128]{1,0:T(8,128)S(1)} %fusion.17), custom_call_target="Cholesky" | custom-call | tf_op jit(solution)/shard_map/jit(cholesky)/cholesky | solution.py:49
  170.0 0.6 compare_reduce_fusion
  170.6 0.7 fusion.12
  171.3 9.8 %custom-call.8 = f32[1,128,128]{1,2,0:T(8,128)S(1)} custom-call(f32[1,128,128]{2,1,0:T(8,128)S(1)} %fusion.12), custom_call_target="InvertDiagBlocksLowerTriangular" | custom-call | tf_op jit(solution)/shard_map/triangular_solve | solution.py:54
  181.1 0.2 fusion.15
  181.3 0.2 fusion.13
  181.5 0.8 fusion.24
  (6 shorter events, 0.1 us)
Async XLA Ops:
  6.5 1.6 copy-start
  6.5 45.8 %all-reduce.4.cloned.1.call-start = ((), (), s32[]{:S(2)}) async-start(), calls=%async_computation | async-start | bytes 1048576 | tf_op jit(solution)/shard_map/psum | solution.py:38
  16.4 90.2 %all-reduce.6.cloned.1.call-start = ((), (), s32[]{:S(2)}) async-start(), calls=%async_computation.1 | async-start | bytes 2097152 | tf_op jit(solution)/shard_map/psum | solution.py:35
  16.5 10.0 %copy-start.1 = (bf16[32,64,1024]{2,1,0:T(8,128)(2,1)S(1)}, bf16[32,64,1024]{2,1,0:T(8,128)(2,1)}, u32[]{:S(2)}) copy-start(bf16[32,64,1024]{2,1,0:T(8,128)(2,1)} %param.9) | copy-start | bytes 12582916
  26.5 3.9 %copy-start.2 = (s32[32,64]{1,0:T(8,128)S(1)}, s32[32,64]{1,0:T(8,128)}, u32[]{:S(2)}) copy-start(s32[32,64]{1,0:T(8,128)} %param.10) | copy-start | bytes 24580
  26.5 3.9 %copy-start.3 = (s32[16,64]{1,0:T(8,128)S(1)}, s32[16,64]{1,0:T(8,128)}, u32[]{:S(2)}) copy-start(s32[16,64]{1,0:T(8,128)} %param.13) | copy-start | bytes 12292
  30.3 124.0 %all-reduce.8.cloned.1.call-start = ((), (), s32[]{:S(2)}) async-start(), calls=%async_computation.2 | async-start | bytes 131072 | tf_op jit(solution)/shard_map/psum | solution.py:44
Sparse Core Ops, SparseCore 0:
  16.5 35.7 all-reduce.3
  54.7 51.8 all-reduce.5
  121.1 33.1 all-reduce.7
where the time goes:
time: 189 us
  waiting for transfers between devices  98 us (52%)
  matrix products  31.9 us (17%)
  other arithmetic  26.2 us (14%)
  between operations  13.9 us (7%)
  blocking collectives  12.5 us (7%)
  local copies, waits for them, and re-layouts  6.23 us (3%)
    psum x1, waiting for transfers between devices, body(): summed = lax.psum(train_terms, 'group')  50.9 us
    psum x1, waiting for transfers between devices, body(): gram = lax.psum(partial_value, 'group')  25.1 us
    psum x1, waiting for transfers between devices, body(): syn_summed = lax.psum(syn_terms, 'dp')  21.9 us
    dot_general x2, matrix products, local_terms(): jnp.dot(hidden.reshape(seqs * length, width), in_rows, preferred_element_...  15.5 us
    another operation x3, other arithmetic, body(): lower = jnp.linalg.cholesky(system)  12.4 us
    another operation x2, other arithmetic, body(): lax.linalg.triangular_solve(lower, first, left_side=True, lower=True, tra...  10.5 us
    dot_general x2, matrix products, make_codes(): jnp.einsum('nta,ntb->nab', weighted, in_proj, precision=lax.Precision.HIG...  7.26 us
    all_gather x1, blocking collectives, body(): every = lax.all_gather(columns, 'dp', axis=0, tiled=True)  7.15 us
  transfers between devices with their start and end apart: 3, of which 3 were waited for; matrix products, arithmetic and copies ran while one was open for 11% of the time, Pallas kernels for 0%

commit v1 on v0

--- a/solution.py
+++ b/solution.py
@@ -1,6 +1,10 @@
+import functools
+
 import jax
 import jax.numpy as jnp
 from jax import lax
+from jax.experimental import pallas as pl
+from jax.experimental.pallas import tpu as pltpu
 from jax.sharding import PartitionSpec as P
 
 damp_ratio = 0.1
@@ -61,6 +65,272 @@
     )
 
 
+MESH = pl.DeviceIdType.MESH
+HIGHEST = lax.Precision.HIGHEST
+
+
+def mm(a, b, contract=((1,), (0,))):
+    return lax.dot_general(
+        a, b, (contract, ((), ())), precision=HIGHEST, preferred_element_type=jnp.float32
+    )
+
+
+def inverse(system, bound):
+    total = system.shape[0]
+    rows = lax.broadcasted_iota(jnp.int32, (total, total), 0)
+    cols = lax.broadcasted_iota(jnp.int32, (total, total), 1)
+    eye = (rows == cols).astype(jnp.float32)
+    trace = jnp.sum(jnp.sum(system * eye, axis=1, keepdims=True), axis=0, keepdims=True)
+    damp = trace * (damp_ratio / total)
+    system = system + damp * eye
+    scale = 2.0 / (trace + 2.0 * damp)
+    error = eye - scale * system
+    value = scale * eye
+    radius = (bound - 1.0) / (bound + 1.0)
+    while radius > 3e-6:
+        step = 2.0 / (2.0 - radius * radius)
+        both = mm(jnp.concatenate([error, value], axis=0), error)
+        value = step * (value + both[total:])
+        error = step * both[:total] - (step - 1.0) * eye
+        radius = radius * radius / (2.0 - radius * radius)
+    return system, value
+
+
+def kernel(
+    dims, th, tg, tm, sh, sg, sm, bi, bo, out,
+    th_v, tg_v, sh_v, sg_v, bi_v, bo_v, ci_v, co_v, wi_v, wo_v, vi_v, vo_v,
+    zs, zr, xs, xr, cs, cr, ps, pr, fs, fr,
+    load_sem, z_send, z_recv, x_send, x_recv, c_send, c_recv, p_send, p_recv, f_send, f_recv,
+):
+    D, G, T, S, L, rank = dims
+    N = D * G
+    half = rank // 2
+    per = half // N
+    d = lax.axis_index("dp")
+    g = lax.axis_index("group")
+    me = d * G + g
+
+    def peer(step):
+        j = lax.rem(me + step, N)
+        return j, {"dp": lax.div(j, G), "group": lax.rem(j, G)}
+
+    def load(src, dst, index):
+        return pltpu.make_async_copy(src, dst, load_sem.at[index])
+
+    def rows_of(ref, place, count):
+        return ref.at[pl.ds(pl.multiple_of(place * count, count), count)]
+
+    basis_loads = [
+        load(rows_of(bi, g, th.shape[1]), bi_v, 0),
+        load(rows_of(bo, g, tg.shape[1]), bo_v, 1),
+        load(rows_of(bi, d, sh.shape[1]), ci_v, 2),
+        load(rows_of(bo, d, sg.shape[1]), co_v, 3),
+    ]
+    order = [("t", s) for s in range(1, G)] + [("s", s) for s in range(1, D)] + [("t", 0), ("s", 0)]
+    loads = []
+    for i, (kind, s) in enumerate(order):
+        if kind == "t":
+            place = lax.rem(g + s, G)
+            pair = (load(rows_of(th, place, T * L), th_v.at[s], 4 + 2 * i),
+                    load(rows_of(tg, place, T * L), tg_v.at[s], 5 + 2 * i))
+        else:
+            place = lax.rem(d + s, D)
+            pair = (load(rows_of(sh, place, S * L), sh_v.at[s], 4 + 2 * i),
+                    load(rows_of(sg, place, S * L), sg_v.at[s], 5 + 2 * i))
+        loads.append(pair)
+
+    def start(i):
+        if i < len(loads):
+            loads[i][0].start()
+            loads[i][1].start()
+
+    depth = 3
+    basis_loads[0].start()
+    basis_loads[1].start()
+    for i in range(depth):
+        start(i)
+        if i == 0:
+            basis_loads[2].start()
+            basis_loads[3].start()
+
+    barrier = pltpu.get_barrier_semaphore()
+
+    def greet(step, carry):
+        pl.semaphore_signal(barrier, inc=1, device_id=peer(step)[1], device_id_type=MESH)
+        return carry
+
+    lax.fori_loop(1, N, greet, 0)
+    cs[:, T:, :] = jnp.zeros((half, cs.shape[1] - T, 2 * rank), jnp.float32)
+
+    def pad(raw, wide, first):
+        value = raw[...]
+        blank = jnp.zeros_like(value)
+        wide[...] = jnp.concatenate([value, blank] if first else [blank, value], axis=1)
+
+    basis_loads[0].wait()
+    pad(bi_v, wi_v, True)
+    basis_loads[1].wait()
+    pad(bo_v, wo_v, False)
+    sends = []
+    for i, (kind, s) in enumerate(order):
+        loads[i][0].wait()
+        loads[i][1].wait()
+        start(i + depth)
+        if kind == "s" and s == min(1, D - 1):
+            basis_loads[2].wait()
+            pad(ci_v, vi_v, True)
+            basis_loads[3].wait()
+            pad(co_v, vo_v, False)
+        if kind == "t":
+            zs[s] = jnp.dot(th_v[s], wi_v[...], preferred_element_type=jnp.float32) + jnp.dot(
+                tg_v[s], wo_v[...], preferred_element_type=jnp.float32)
+        else:
+            xs[s] = jnp.dot(sh_v[s], vi_v[...], preferred_element_type=jnp.float32) + jnp.dot(
+                sg_v[s], vo_v[...], preferred_element_type=jnp.float32)
+        if i == 0:
+            pl.semaphore_wait(barrier, N - 1)
+        if s > 0:
+            if kind == "t":
+                copy = pltpu.make_async_remote_copy(
+                    src_ref=zs.at[s], dst_ref=zr.at[s], send_sem=z_send.at[s], recv_sem=z_recv.at[s],
+                    device_id={"group": lax.rem(g + s, G)}, device_id_type=MESH)
+            else:
+                copy = pltpu.make_async_remote_copy(
+                    src_ref=xs.at[s], dst_ref=xr.at[s], send_sem=x_send.at[s], recv_sem=x_recv.at[s],
+                    device_id={"dp": lax.rem(d + s, D)}, device_id_type=MESH)
+            copy.start()
+            sends.append((kind, copy))
+
+    def codes(kind, own, received, mask, count, peers, place, first):
+        for k, copy in sends:
+            if k == kind:
+                copy.wait_recv()
+        for n in range(count):
+            rows = pl.ds(n * L, L)
+            total = own[0, rows, :]
+            for s in range(1, peers):
+                total = total + received[s, rows, :]
+            turned = total.T
+            keep = mask[pl.ds(place * count + n, 1), :].astype(jnp.float32)
+            code = mm(turned[rank:] * keep, total[:, :rank])
+            cs[:, first + n, :] = jnp.concatenate([code[:half], code[half:]], axis=1)
+
+    codes("s", xs, xr, sm, S, D, d, T)
+    codes("t", zs, zr, tm, T, G, g, 0)
+
+    def exchange(source, landing, send_sem, recv_sem):
+        def copy(step, slot):
+            j, where = peer(step)
+            return pltpu.make_async_remote_copy(
+                src_ref=source(j), dst_ref=landing.at[slot], send_sem=send_sem.at[step],
+                recv_sem=recv_sem.at[slot], device_id=where, device_id_type=MESH)
+
+        def send(step, carry):
+            copy(step, me).start()
+            return carry
+
+        def arrive(step, carry):
+            copy(step, lax.rem(me + N - step, N)).wait_recv()
+            return carry
+
+        def left(step, carry):
+            copy(step, me).wait_send()
+            return carry
+
+        lax.fori_loop(1, N, send, 0)
+        yield
+        lax.fori_loop(1, N, arrive, 0)
+        yield
+        lax.fori_loop(1, N, left, 0)
+        yield
+
+    R = cs.shape[1]
+    swap = exchange(lambda j: cs.at[pl.ds(j * per, per)], cr, c_send, c_recv)
+    next(swap)
+    cr[me] = cs[pl.ds(me * per, per)]
+    next(swap)
+    train = jnp.concatenate([cr[:, p, :T, :].reshape(N * T, 2 * rank) for p in range(per)], axis=1)
+    syn = jnp.concatenate([cr[:, p, T:, :].reshape(N * (R - T), 2 * rank) for p in range(per)], axis=1)
+    product = mm(jnp.concatenate([train, syn], axis=0), train, ((1,), (1,)))
+    ps[:, :T, :] = product[: N * T].reshape(N, T, N * T)
+    ps[:, T:, :] = product[N * T :].reshape(N, R - T, N * T)
+    reduce = exchange(lambda j: ps.at[j], pr, p_send, p_recv)
+    next(reduce)
+    pr[me] = ps[me]
+    next(reduce)
+    mine = pr[0]
+    for j in range(1, N):
+        mine = mine + pr[j]
+    fs[...] = mine
+    gather = exchange(lambda j: fs, fr, f_send, f_recv)
+    next(gather)
+    fr[me] = mine
+    next(gather)
+    gram = fr[:, :T, :].reshape(N * T, N * T)
+    raw = jnp.concatenate([fr[p * G + g, T:, :] for p in range(D)], axis=0)
+    system, value = inverse(gram, 1.0 + N * T / damp_ratio)
+    scores = mm(raw, value)
+    scores = scores + mm(raw - mm(scores, system), value)
+    for p in range(D):
+        out[pl.ds(p * S, S), :] = scores[p * (R - T) : p * (R - T) + S]
+    for k, copy in sends:
+        copy.wait_send()
+    next(swap)
+    next(reduce)
+    next(gather)
+
+
+def fused(D, G, th, tg, tm, sh, sg, sm, bi, bo):
+    rank = bi.shape[1]
+    L = th.shape[1]
+    T, S = th.shape[0] // G, sh.shape[0] // D
+    N = D * G
+    R = T + 8 * ((S + 7) // 8)
+    total = N * T
+    per = rank // 2 // N
+    f32, bf16 = jnp.float32, jnp.bfloat16
+    flat = lambda x: x.reshape(x.shape[0] * x.shape[1], x.shape[2])
+    ins, outs, sins, souts = th.shape[2], tg.shape[2], sh.shape[2], sg.shape[2]
+    dma = lambda n: pltpu.SemaphoreType.DMA((n,))
+    anywhere = pl.BlockSpec(memory_space=pl.ANY)
+    local = pl.BlockSpec(memory_space=pltpu.VMEM)
+    scores = pl.pallas_call(
+        functools.partial(kernel, (D, G, T, S, L, rank)),
+        out_shape=jax.ShapeDtypeStruct((D * S, total), f32),
+        in_specs=[anywhere, anywhere, local, anywhere, anywhere, local, anywhere, anywhere],
+        out_specs=local,
+        scratch_shapes=[
+            pltpu.VMEM((G, T * L, ins), bf16), pltpu.VMEM((G, T * L, outs), bf16),
+            pltpu.VMEM((D, S * L, sins), bf16), pltpu.VMEM((D, S * L, souts), bf16),
+            pltpu.VMEM((ins, rank), bf16), pltpu.VMEM((outs, rank), bf16),
+            pltpu.VMEM((sins, rank), bf16), pltpu.VMEM((souts, rank), bf16),
+            pltpu.VMEM((ins, 2 * rank), bf16), pltpu.VMEM((outs, 2 * rank), bf16),
+            pltpu.VMEM((sins, 2 * rank), bf16), pltpu.VMEM((souts, 2 * rank), bf16),
+            pltpu.VMEM((G, T * L, 2 * rank), f32), pltpu.VMEM((G, T * L, 2 * rank), f32),
+            pltpu.VMEM((D, S * L, 2 * rank), f32), pltpu.VMEM((D, S * L, 2 * rank), f32),
+            pltpu.VMEM((rank // 2, R, 2 * rank), f32), pltpu.VMEM((N, per, R, 2 * rank), f32),
+            pltpu.VMEM((N, R, total), f32), pltpu.VMEM((N, R, total), f32),
+            pltpu.VMEM((R, total), f32), pltpu.VMEM((N, R, total), f32),
+            dma(4 + 2 * (G + D)), dma(G), dma(G), dma(D), dma(D),
+            dma(N), dma(N), dma(N), dma(N), dma(N), dma(N),
+        ],
+        compiler_params=pltpu.CompilerParams(
+            collective_id=0, has_side_effects=True, vmem_limit_bytes=56 * 1024 * 1024
+        ),
+        cost_estimate=pl.CostEstimate(flops=2 * 10**9, bytes_accessed=30 * 10**6, transcendentals=0),
+    )(flat(th), flat(tg), tm, flat(sh), flat(sg), sm, bi, bo)
+    width = total // D
+    return lax.dynamic_slice_in_dim(scores, lax.axis_index("dp") * width, width, 1)
+
+
+def fits(D, G, train, syn, rank):
+    N = D * G
+    return (
+        train % (8 * N) == 0 and train // N == 8 and syn % N == 0 and syn // N <= 8
+        and rank == 64 and (rank // 2) % N == 0
+    )
+
+
 def solution(mesh):
     placed = (
         P(("parts", "dp"), None, "group"),
@@ -72,6 +342,14 @@
         P(),
         P(),
     )
+    D, G = mesh.shape["dp"], mesh.shape["group"]
+
+    def local(*args):
+        train, syn, rank = args[0].shape[0] * D, args[3].shape[0] * G, args[6].shape[1]
+        if fits(D, G, train, syn, rank):
+            return fused(D, G, *args)
+        return body(*args)
+
     return jax.shard_map(
-        body, mesh=mesh, in_specs=placed, out_specs=P(("parts", "group"), "dp"), check_vma=False
-    )
+        local, mesh=mesh, in_specs=placed, out_specs=P(("parts", "group"), "dp"), check_vma=False
+    )

time: 189 us -> 63.6 us (0.34)
  waiting for transfers between devices: 98 us -> 0 us
  Pallas kernels: 0 us -> 55.9 us
  matrix products: 31.9 us -> 0 us
  other arithmetic: 26.2 us -> 0 us
  between operations: 13.9 us -> 0.02 us
  blocking collectives: 12.5 us -> 0 us
    psum x3 -> x0, waiting for transfers between devices: 97.9 us -> none  [the longest x1 50.9 us: body(): summed = lax.psum(train_terms, 'group')]
    pallas_call x0 -> x1, Pallas kernels: none -> 55.9 us  [fused(): pl.pallas_call(functools.partial(kernel, (D, G, T, S, L, rank)), out_shap...]
    dot_general x9 -> x0, matrix products: 31.5 us -> none  [the longest x2 15.5 us: local_terms(): jnp.dot(hidden.reshape(seqs * length, width), in_rows, preferred_element_...]
    another operation x5 -> x0, other arithmetic: 22.9 us -> none  [the longest x3 12.4 us: body(): lower = jnp.linalg.cholesky(system)]
    all_gather x2 -> x0, blocking collectives: 12.5 us -> none  [the longest x1 7.15 us: body(): every = lax.all_gather(columns, 'dp', axis=0, tiled=True)]
    unnamed x9 -> x4, local copies, waits for them, and re-layouts: 1.69 us -> 5.94 us
    concatenate x2 -> x0, local copies, waits for them, and re-layouts: 2.37 us -> none  [local_terms(): jnp.concatenate([in_proj, out_proj], axis=1).reshape(seqs, length, -1)]
  transfers between devices with their start and end apart: 3 -> 0, of which waited for: 3 -> 0; matrix products, arithmetic and copies ran while one was open for 11% -> 0% of each run, Pallas kernels for 0% -> 0%
where the time goes in v1:
time: 63.6 us; the launch traced here: 63.2 us
  Pallas kernels  55.9 us (88%)
  local copies, waits for them, and re-layouts  7.31 us (11%)
    pallas_call x1, Pallas kernels, fused(): pl.pallas_call(functools.partial(kernel, (D, G, T, S, L, rank)), out_shap...  55.9 us
    unnamed x4, local copies, waits for them, and re-layouts  5.94 us
    dynamic_slice x1, local copies, waits for them, and re-layouts, fused(): lax.dynamic_slice_in_dim(scores, lax.axis_index('dp') * width, width, 1)  1.37 us

profile of v1, /device:TPU:0, one launch (start us, length us, event | category | flops | bytes accessed | tf_op | source)
XLA Modules:
  0.0 63.2 jit_solution(16150119886072539055)
XLA Ops:
  0.0 0.0 copy-start
  0.0 4.6 %copy.9.bi = bf16[14336,64]{1,0:T(8,128)(2,1)} copy(bf16[14336,64]{0,1:T(8,128)(2,1)} %param.14) | data formatting | bytes 3670016 | tf_op args[6]
  4.6 0.0 copy-done
  4.6 1.3 %copy.10.bo = bf16[4096,64]{1,0:T(8,128)(2,1)} copy(bf16[4096,64]{0,1:T(8,128)(2,1)S(1)} %copy-done) | data formatting | bytes 1048576 | tf_op args[7]
  5.9 55.9 %shard_map.82 = f32[16,128]{1,0:T(8,128)} custom-call(bf16[2048,3584]{1,0:T(8,128)(2,1)} %bitcast.4, bf16[2048,1024]{1,0:T(8,128)(2,1)} %bitcast.6, s32[32,64]{1,0:T(8,128)} %tm.1, bf16[1024,3584]{1,0:T(8,128)(2,1)} %bitcast.5, bf16[1024,1024]{1,0:T(8,128)(2,1)} %bitcast.7, s32[16,64]{1,0:T(8,128)} %sm.1, bf16[14336,64]{1,0:T(8,128)(2,1)} %copy.9.bi, ...), custom_call_target="tpu_custom_call" | custom-call | flops 2000000000 | bytes 30000000 | tf_op jit(solution)/shard_map/pallas_call | solution.py:297
  61.9 1.4 %constant_dynamic-slice_fusion = f32[16,32]{1,0:T(8,128)} fusion(f32[16,128]{1,0:T(8,128)} %shard_map.82, s32[]{:T(128)S(6)} %select_n.3), kind=kLoop, calls=%fused_computation | loop fusion | bytes 4100 | tf_op jit(solution)/shard_map/dynamic_slice | solution.py:323
Async XLA Ops:
  0.0 4.6 %copy-start = (bf16[4096,64]{0,1:T(8,128)(2,1)S(1)}, bf16[4096,64]{0,1:T(8,128)(2,1)}, u32[]{:S(2)}) copy-start(bf16[4096,64]{0,1:T(8,128)(2,1)} %param.15) | copy-start | bytes 1572868

commit v2 on v1

--- a/solution.py
+++ b/solution.py
@@ -98,7 +98,7 @@
 
 def kernel(
     dims, th, tg, tm, sh, sg, sm, bi, bo, out,
-    th_v, tg_v, sh_v, sg_v, bi_v, bo_v, ci_v, co_v, wi_v, wo_v, vi_v, vo_v,
+    th_v, tg_v, sh_v, sg_v, bi_v, bo_v, ci_v, co_v,
     zs, zr, xs, xr, cs, cr, ps, pr, fs, fr,
     load_sem, z_send, z_recv, x_send, x_recv, c_send, c_recv, p_send, p_recv, f_send, f_recv,
 ):
@@ -120,17 +120,29 @@
     def rows_of(ref, place, count):
         return ref.at[pl.ds(pl.multiple_of(place * count, count), count)]
 
+    def columns_of(ref, place, count):
+        return ref.at[:, pl.ds(pl.multiple_of(place * count, count), count)]
+
+    low = 2 * g < G
+
+    def target(i):
+        near = jnp.where(low, g, G - 1 - g)
+        far = G - 1 - near
+        place = near if i == G - 1 else jnp.where(i < far, G - 1 - i, i - far)
+        return jnp.where(low, place, G - 1 - place)
+
     basis_loads = [
-        load(rows_of(bi, g, th.shape[1]), bi_v, 0),
-        load(rows_of(bo, g, tg.shape[1]), bo_v, 1),
-        load(rows_of(bi, d, sh.shape[1]), ci_v, 2),
-        load(rows_of(bo, d, sg.shape[1]), co_v, 3),
+        load(columns_of(bi, g, th.shape[1]), bi_v, 0),
+        load(columns_of(bo, g, tg.shape[1]), bo_v, 1),
+        load(columns_of(bi, d, sh.shape[1]), ci_v, 2),
+        load(columns_of(bo, d, sg.shape[1]), co_v, 3),
     ]
-    order = [("t", s) for s in range(1, G)] + [("s", s) for s in range(1, D)] + [("t", 0), ("s", 0)]
+    targets = [target(i) for i in range(G)]
+    order = [("t", i) for i in range(G)] + [("s", s) for s in range(1, D)] + [("s", 0)]
     loads = []
     for i, (kind, s) in enumerate(order):
         if kind == "t":
-            place = lax.rem(g + s, G)
+            place = targets[s]
             pair = (load(rows_of(th, place, T * L), th_v.at[s], 4 + 2 * i),
                     load(rows_of(tg, place, T * L), tg_v.at[s], 5 + 2 * i))
         else:
@@ -160,63 +172,96 @@
         return carry
 
     lax.fori_loop(1, N, greet, 0)
-    cs[:, T:, :] = jnp.zeros((half, cs.shape[1] - T, 2 * rank), jnp.float32)
-
-    def pad(raw, wide, first):
-        value = raw[...]
-        blank = jnp.zeros_like(value)
-        wide[...] = jnp.concatenate([value, blank] if first else [blank, value], axis=1)
+
+    def project(basis, chunk):
+        return lax.dot_general(
+            basis, chunk, (((1,), (1,)), ((), ())), preferred_element_type=jnp.float32)
+
+    edge = (g == 0) | (g == G - 1)
+
+    def onward(t):
+        right = t > g
+        slot = jnp.where(right | (t != g - 1), t, G)
+        return pltpu.make_async_remote_copy(
+            src_ref=zs.at[t], dst_ref=zr.at[slot], send_sem=z_send.at[t], recv_sem=z_recv.at[slot],
+            device_id={"group": jnp.where(right, jnp.minimum(g + 1, G - 1), jnp.maximum(g - 1, 0))},
+            device_id_type=MESH)
+
+    def landed(slot):
+        pltpu.make_async_remote_copy(
+            src_ref=zs.at[0], dst_ref=zr.at[slot], send_sem=z_send.at[0], recv_sem=z_recv.at[slot],
+            device_id={"group": jnp.where(g > 0, g - 1, g + 1)}, device_id_type=MESH).wait_recv()
+
+    def forward(i):
+        t = targets[i]
+
+        @pl.when(jnp.logical_not(edge))
+        def _():
+            landed(t)
+            zs[t] = zs[t] + zr[t]
+            onward(t).start()
 
     basis_loads[0].wait()
-    pad(bi_v, wi_v, True)
     basis_loads[1].wait()
-    pad(bo_v, wo_v, False)
     sends = []
     for i, (kind, s) in enumerate(order):
         loads[i][0].wait()
         loads[i][1].wait()
         start(i + depth)
-        if kind == "s" and s == min(1, D - 1):
-            basis_loads[2].wait()
-            pad(ci_v, vi_v, True)
-            basis_loads[3].wait()
-            pad(co_v, vo_v, False)
         if kind == "t":
-            zs[s] = jnp.dot(th_v[s], wi_v[...], preferred_element_type=jnp.float32) + jnp.dot(
-                tg_v[s], wo_v[...], preferred_element_type=jnp.float32)
+            t = targets[s]
+            zs[t, :rank] = project(bi_v[...], th_v[s])
+            zs[t, rank:] = project(bo_v[...], tg_v[s])
+            if i == 0:
+                pl.semaphore_wait(barrier, N - 1)
+            if s < G - 1:
+                pl.when(edge)(lambda: onward(t).start())
         else:
-            xs[s] = jnp.dot(sh_v[s], vi_v[...], preferred_element_type=jnp.float32) + jnp.dot(
-                sg_v[s], vo_v[...], preferred_element_type=jnp.float32)
-        if i == 0:
-            pl.semaphore_wait(barrier, N - 1)
-        if s > 0:
-            if kind == "t":
-                copy = pltpu.make_async_remote_copy(
-                    src_ref=zs.at[s], dst_ref=zr.at[s], send_sem=z_send.at[s], recv_sem=z_recv.at[s],
-                    device_id={"group": lax.rem(g + s, G)}, device_id_type=MESH)
-            else:
+            if i == G:
+                basis_loads[2].wait()
+                basis_loads[3].wait()
+                forward(0)
+            xs[s, :rank] = project(ci_v[...], sh_v[s])
+            xs[s, rank:] = project(co_v[...], sg_v[s])
+            if s > 0:
                 copy = pltpu.make_async_remote_copy(
                     src_ref=xs.at[s], dst_ref=xr.at[s], send_sem=x_send.at[s], recv_sem=x_recv.at[s],
                     device_id={"dp": lax.rem(d + s, D)}, device_id_type=MESH)
-            copy.start()
-            sends.append((kind, copy))
-
-    def codes(kind, own, received, mask, count, peers, place, first):
-        for k, copy in sends:
-            if k == kind:
-                copy.wait_recv()
-        for n in range(count):
-            rows = pl.ds(n * L, L)
-            total = own[0, rows, :]
-            for s in range(1, peers):
-                total = total + received[s, rows, :]
-            turned = total.T
-            keep = mask[pl.ds(place * count + n, 1), :].astype(jnp.float32)
-            code = mm(turned[rank:] * keep, total[:, :rank])
-            cs[:, first + n, :] = jnp.concatenate([code[:half], code[half:]], axis=1)
-
-    codes("s", xs, xr, sm, S, D, d, T)
-    codes("t", zs, zr, tm, T, G, g, 0)
+                copy.start()
+                sends.append(copy)
+
+    def codes(total, mask, count, place, first):
+        lanes = lax.broadcasted_iota(jnp.int32, (1, 2 * L), 1)
+        for n in range(0, count, 2):
+            both = total(pl.ds(n * L, 2 * L))
+            keep = jnp.concatenate(
+                [mask[pl.ds(place * count + n, 1), :], mask[pl.ds(place * count + n + 1, 1), :]], axis=1
+            ).astype(jnp.float32)
+            left = jnp.where(lanes < L, keep, 0.0)
+            right = jnp.where(lanes < L, 0.0, keep)
+            weighted = jnp.concatenate([both[rank:] * left, both[rank:] * right], axis=0)
+            pair = mm(weighted, both[:rank], ((1,), (1,)))
+            for k in range(2):
+                code = pair[k * rank : (k + 1) * rank]
+                cs[:, first + n + k, :] = jnp.concatenate([code[:half], code[half:]], axis=1)
+
+    for i in range(1, G - 1):
+        forward(i)
+    for copy in sends:
+        copy.wait_recv()
+    codes(lambda c: sum((xr[s, :, c] for s in range(1, D)), xs[0, :, c]), sm, S, d, T)
+
+    @pl.when(g > 0)
+    def _():
+        landed(g)
+        zs[g] = zs[g] + zr[g]
+
+    @pl.when(g < G - 1)
+    def _():
+        landed(G)
+        zs[g] = zs[g] + zr[G]
+
+    codes(lambda c: zs[g, :, c], tm, T, g, 0)
 
     def exchange(source, landing, send_sem, recv_sem):
         def copy(step, slot):
@@ -271,10 +316,15 @@
     system, value = inverse(gram, 1.0 + N * T / damp_ratio)
     scores = mm(raw, value)
     scores = scores + mm(raw - mm(scores, system), value)
-    for p in range(D):
-        out[pl.ds(p * S, S), :] = scores[p * (R - T) : p * (R - T) + S]
-    for k, copy in sends:
+    width = out.shape[1]
+    chosen = scores[:, :width]
+    for p in range(1, D):
+        chosen = jnp.where(d == p, scores[:, p * width : (p + 1) * width], chosen)
+    out[...] = chosen
+    for copy in sends:
         copy.wait_send()
+    for i in range(G - 1):
+        onward(targets[i]).wait_send()
     next(swap)
     next(reduce)
     next(gather)
@@ -285,7 +335,7 @@
     L = th.shape[1]
     T, S = th.shape[0] // G, sh.shape[0] // D
     N = D * G
-    R = T + 8 * ((S + 7) // 8)
+    R = T + S
     total = N * T
     per = rank // 2 // N
     f32, bf16 = jnp.float32, jnp.bfloat16
@@ -294,40 +344,36 @@
     dma = lambda n: pltpu.SemaphoreType.DMA((n,))
     anywhere = pl.BlockSpec(memory_space=pl.ANY)
     local = pl.BlockSpec(memory_space=pltpu.VMEM)
-    scores = pl.pallas_call(
+    return pl.pallas_call(
         functools.partial(kernel, (D, G, T, S, L, rank)),
-        out_shape=jax.ShapeDtypeStruct((D * S, total), f32),
+        out_shape=jax.ShapeDtypeStruct((D * S, total // D), f32),
         in_specs=[anywhere, anywhere, local, anywhere, anywhere, local, anywhere, anywhere],
         out_specs=local,
         scratch_shapes=[
             pltpu.VMEM((G, T * L, ins), bf16), pltpu.VMEM((G, T * L, outs), bf16),
             pltpu.VMEM((D, S * L, sins), bf16), pltpu.VMEM((D, S * L, souts), bf16),
-            pltpu.VMEM((ins, rank), bf16), pltpu.VMEM((outs, rank), bf16),
-            pltpu.VMEM((sins, rank), bf16), pltpu.VMEM((souts, rank), bf16),
-            pltpu.VMEM((ins, 2 * rank), bf16), pltpu.VMEM((outs, 2 * rank), bf16),
-            pltpu.VMEM((sins, 2 * rank), bf16), pltpu.VMEM((souts, 2 * rank), bf16),
-            pltpu.VMEM((G, T * L, 2 * rank), f32), pltpu.VMEM((G, T * L, 2 * rank), f32),
-            pltpu.VMEM((D, S * L, 2 * rank), f32), pltpu.VMEM((D, S * L, 2 * rank), f32),
+            pltpu.VMEM((rank, ins), bf16), pltpu.VMEM((rank, outs), bf16),
+            pltpu.VMEM((rank, sins), bf16), pltpu.VMEM((rank, souts), bf16),
+            pltpu.VMEM((G, 2 * rank, T * L), f32), pltpu.VMEM((G + 1, 2 * rank, T * L), f32),
+            pltpu.VMEM((D, 2 * rank, S * L), f32), pltpu.VMEM((D, 2 * rank, S * L), f32),
             pltpu.VMEM((rank // 2, R, 2 * rank), f32), pltpu.VMEM((N, per, R, 2 * rank), f32),
             pltpu.VMEM((N, R, total), f32), pltpu.VMEM((N, R, total), f32),
             pltpu.VMEM((R, total), f32), pltpu.VMEM((N, R, total), f32),
-            dma(4 + 2 * (G + D)), dma(G), dma(G), dma(D), dma(D),
+            dma(4 + 2 * (G + D)), dma(G), dma(G + 1), dma(D), dma(D),
             dma(N), dma(N), dma(N), dma(N), dma(N), dma(N),
         ],
         compiler_params=pltpu.CompilerParams(
             collective_id=0, has_side_effects=True, vmem_limit_bytes=56 * 1024 * 1024
         ),
         cost_estimate=pl.CostEstimate(flops=2 * 10**9, bytes_accessed=30 * 10**6, transcendentals=0),
-    )(flat(th), flat(tg), tm, flat(sh), flat(sg), sm, bi, bo)
-    width = total // D
-    return lax.dynamic_slice_in_dim(scores, lax.axis_index("dp") * width, width, 1)
+    )(flat(th), flat(tg), tm, flat(sh), flat(sg), sm, bi.T, bo.T)
 
 
 def fits(D, G, train, syn, rank):
     N = D * G
     return (
         train % (8 * N) == 0 and train // N == 8 and syn % N == 0 and syn // N <= 8
-        and rank == 64 and (rank // 2) % N == 0
+        and syn // N % 2 == 0 and G > 1 and D > 1 and 2 * rank % 128 == 0 and (rank // 2) % N == 0
     )
 
 

time: 63.6 us -> 50 us (0.79)
  Pallas kernels: 55.9 us -> 48.4 us
  local copies, waits for them, and re-layouts: 7.31 us -> 1.3 us
    pallas_call x1, Pallas kernels: 55.9 us -> 48.4 us  [fused(): pl.pallas_call(functools.partial(kernel, (D, G, T, S, L, rank)), out_shap...]
    unnamed x4 -> x1, local copies, waits for them, and re-layouts: 5.94 us -> 1.3 us
    dynamic_slice x1 -> x0, local copies, waits for them, and re-layouts: 1.37 us -> none  [fused(): lax.dynamic_slice_in_dim(scores, lax.axis_index('dp') * width, width, 1)]
where the time goes in v2:
time: 50 us; the launch traced here: 49.7 us
  Pallas kernels  48.4 us (97%)
  local copies, waits for them, and re-layouts  1.3 us (3%)
    pallas_call x1, Pallas kernels, fused(): pl.pallas_call(functools.partial(kernel, (D, G, T, S, L, rank)), out_shap...  48.4 us
    unnamed x1, local copies, waits for them, and re-layouts  1.3 us

profile of v2, /device:TPU:0, one launch (start us, length us, event | category | flops | bytes accessed | tf_op | source)
XLA Modules:
  0.0 49.7 jit_solution(17561775464679460726)
XLA Ops:
  0.0 48.4 %shard_map.82 = f32[16,32]{1,0:T(8,128)} custom-call(bf16[2048,3584]{1,0:T(8,128)(2,1)} %bitcast.6, bf16[2048,1024]{1,0:T(8,128)(2,1)} %bitcast.8, s32[32,64]{1,0:T(8,128)} %tm.1, bf16[1024,3584]{1,0:T(8,128)(2,1)} %bitcast.7, bf16[1024,1024]{1,0:T(8,128)(2,1)} %bitcast.9, s32[16,64]{1,0:T(8,128)} %sm.1, bf16[64,14336]{1,0:T(8,128)(2,1)} %bitcast.10, ...), custom_call_target="tpu_custom_call" | custom-call | flops 2000000000 | bytes 30000000 | tf_op jit(solution)/shard_map/pallas_call | solution.py:347
  48.4 1.3 %copy.10 = f32[16,32]{1,0:T(8,128)} copy(f32[16,32]{1,0:T(8,128)} %shard_map.82) | data formatting | bytes 4096
